TPU v7x, 32 devices: a whole 2x2x4 slice. The times are simulated.
32 devices in a mesh: gx: 4 (over z), gy: 8 (over y, x, core).
Axes of the slice: x: 2, y: 2, z: 4, core: 2. Of those that a mesh axis runs over, the one named last changes fastest.
Arguments:
- position: float32 [3, 32, 64, 128], P(None, 'gx', 'gy'), may hold values from 0 to 1
- velocity: float32 [3, 32, 64, 128], P(None, 'gx', 'gy'), may hold values from -4 to 4
- history: float32 [3, 32, 64, 128], P(None, 'gx', 'gy'), may hold values from -4 to 4
- radius: float32 [32, 64, 128], P('gx', 'gy'), may hold values from 0.06 to 0.09
- fluid: float32 [3, 32, 64, 128], P(None, 'gx', 'gy'), may hold values from -6 to 6
- tile_list: int32 [32, 64, 4], P('gx', 'gy'), may hold values from 0 to 7, all different within a row
- tile_mask: int32 [32, 64, 4], P('gx', 'gy'), may hold values from 0 to 1
- move_slot: int32 [4, 32, 64, 64], P(None, 'gx', 'gy'), may hold values from 0 to 127, as said below
Outputs:
- position_out: float32 [3, 32, 64, 128], P(None, 'gx', 'gy')
- velocity_out: float32 [3, 32, 64, 128], P(None, 'gx', 'gy')
- history_out: float32 [3, 32, 64, 128], P(None, 'gx', 'gy')
Inputs may be any that keep to these rules, and one draw needn't show every extreme that they name: `move_slot`: within a block and substep the 64 slots are distinct.
All inputs are finite; a program needn't handle non-finite values.
Results may differ from a plain program's by a relative error of at most 0.0003.
Values sent between devices are 32-bit elements; how exact they have to be, the bound alone decides.
A program may use at most 64 MiB of HBM per device.

v0:
```python
import jax
import jax.numpy as jnp
import numpy as np
from jax import lax
from jax.sharding import PartitionSpec as P

time_step = 0.05
normal_stiff = 50.0
shear_stiff = 40.0
drag_rate = 2.0
gravity = 1.0
floor_square = 0.0025
base_radius = 0.075
shift_first = np.array([offset // 3 - 1 for offset in range(9)], np.float32)
shift_second = np.array([offset % 3 - 1 for offset in range(9)], np.float32)


def from_behind(value, axis, steps):
    count = lax.axis_size(axis)
    first, last = (max(0, -steps), min(count, count - steps))
    return lax.ppermute(value, axis, [(source, source + steps) for source in range(first, last)])


def padded_2(x, sides, width):
    for axis, dim in sides:
        count, length = (lax.axis_size(axis), x.shape[dim])
        up = [(i, (i + 1) % count) for i in range(count - 1)]
        down = [(j, i) for i, j in up]
        last = lax.slice_in_dim(x, length - width, length, axis=dim)
        first = lax.slice_in_dim(x, 0, width, axis=dim)
        before = lax.ppermute(last, axis, up)
        after = lax.ppermute(first, axis, down)
        x = jnp.concatenate([before, x, after], axis=dim)
    return x


def pair_forces(home, partner, offset_vec, weight, pair_mask):
    home_pos, home_his, home_rad = (home[0:3], home[3:6], home[6])
    far_pos, far_his, far_rad = (partner[0:3], partner[3:6], partner[6])
    delta = far_pos[:, :, None, :] + offset_vec[:, :, None, None] - home_pos[:, :, :, None]
    dist_sq = jnp.sum(delta * delta, axis=0)
    distance = jnp.sqrt(jnp.maximum(dist_sq, floor_square))
    present = (far_rad > 0.0).astype(jnp.float32)
    intersection = jnp.maximum(home_rad[:, :, None] + far_rad[:, None, :] - distance, 0.0)
    intersection = intersection * present[:, None, :] * weight[:, None, None] * pair_mask
    pushing = jnp.sum(intersection[None] * delta / distance[None], axis=3)
    loading = jnp.sum(intersection, axis=2)
    spring = jnp.einsum("bij,cbj->cbi", intersection, far_his, precision=lax.Precision.HIGHEST)
    return -normal_stiff * pushing - shear_stiff * (home_his * loading[None] - spring)


def row_force(window, tile_row, mask_row):
    home = window[:, 1, 1:-1]
    width = home.shape[1]
    grains = home.shape[2]
    views = jnp.stack(
        [window[:, offset // 3, offset % 3 : offset % 3 + width] for offset in range(9)]
    )
    zero_vec = jnp.zeros((3, width), jnp.float32)
    self_mask = 1.0 - jnp.eye(grains, dtype=jnp.float32)
    total = pair_forces(home, home, zero_vec, jnp.ones((width,), jnp.float32), self_mask)
    picked = tile_row + (tile_row >= 4).astype(jnp.int32)
    onehot = (picked[:, :, None] == jnp.arange(9, dtype=jnp.int32)[None, None, :]).astype(
        jnp.float32
    )
    weights = mask_row.astype(jnp.float32)
    for slot_k in range(tile_row.shape[1]):
        select = onehot[:, slot_k].T
        partner = jnp.sum(select[:, None, :, None] * views, axis=0)
        along_one = jnp.sum(select * jnp.asarray(shift_first)[:, None], axis=0)
        along_two = jnp.sum(select * jnp.asarray(shift_second)[:, None], axis=0)
        offset_vec = jnp.stack([along_one, along_two, jnp.zeros_like(along_one)])
        total = total + pair_forces(home, partner, offset_vec, weights[:, slot_k], 1.0)
    return total


def all_forces(padded, tile_list, tile_mask):
    rows = padded.shape[1] - 2

    def one_row(row_index):
        window = lax.dynamic_slice_in_dim(padded, row_index, 3, axis=1)
        return row_force(window, tile_list[row_index], tile_mask[row_index])

    result = lax.map(one_row, jnp.arange(rows, dtype=jnp.int32))
    return jnp.moveaxis(result, 0, 1)


def advance(position, velocity, history, radius, fluid, force):
    vertical = jnp.array([0.0, 0.0, 1.0], jnp.float32).reshape(3, 1, 1, 1)
    lift = normal_stiff * jnp.maximum(radius - position[2], 0.0)
    force = force + lift[None] * vertical
    mass = (radius / base_radius) ** 3
    accel = force / mass[None] + drag_rate * (fluid - velocity) - gravity * vertical
    velocity = velocity + time_step * accel
    history = history + time_step * velocity
    position = position + time_step * velocity
    return (position, velocity, history)


def slot_table(group, grains):
    return (group[..., None] == jnp.arange(grains, dtype=jnp.int32)).astype(jnp.float32)


def pick_slots(state, table):
    return jnp.einsum("cabg,abkg->cabk", state, table, precision=lax.Precision.HIGHEST)


def place(state, table, values):
    covered = jnp.sum(table, axis=2)
    added = jnp.einsum("cabk,abkg->cabg", values, table, precision=lax.Precision.HIGHEST)
    return state * (1.0 - covered)[None] + added


def unit_channel(which):
    return (jnp.arange(10) == which).astype(jnp.float32).reshape(10, 1, 1, 1)


def migrate(state, slots):
    count = slots.shape[-1] // 4
    grains = state.shape[3]
    tables = [
        slot_table(slots[..., part_k * count : (part_k + 1) * count], grains) for part_k in range(4)
    ]
    packets = [pick_slots(state, table) for table in tables]
    first_unit = unit_channel(0)
    second_unit = unit_channel(1)
    index_x = lax.axis_index("gx")
    index_y = lax.axis_index("gy")
    size_x = lax.axis_size("gx")
    size_y = lax.axis_size("gy")
    from_behind_x = from_behind(packets[0][:, -1], "gx", 1)
    from_ahead_x = from_behind(packets[1][:, 0], "gx", -1)
    from_behind_y = from_behind(packets[2][:, :, -1], "gy", 1)
    from_ahead_y = from_behind(packets[3][:, :, 0], "gy", -1)
    edge_minus_x = jnp.where(index_x == 0, packets[1][:, 0], from_behind_x - first_unit[:, 0])
    edge_plus_x = jnp.where(
        index_x == size_x - 1, packets[0][:, -1], from_ahead_x + first_unit[:, 0]
    )
    edge_minus_y = jnp.where(
        index_y == 0, packets[3][:, :, 0], from_behind_y - second_unit[:, :, 0]
    )
    edge_plus_y = jnp.where(
        index_y == size_y - 1, packets[2][:, :, -1], from_ahead_y + second_unit[:, :, 0]
    )
    into_minus_x = jnp.concatenate([edge_minus_x[:, None], packets[0][:, :-1] - first_unit], axis=1)
    into_plus_x = jnp.concatenate([packets[1][:, 1:] + first_unit, edge_plus_x[:, None]], axis=1)
    into_minus_y = jnp.concatenate(
        [edge_minus_y[:, :, None], packets[2][:, :, :-1] - second_unit], axis=2
    )
    into_plus_y = jnp.concatenate(
        [packets[3][:, :, 1:] + second_unit, edge_plus_y[:, :, None]], axis=2
    )
    state = place(state, tables[1], into_minus_x)
    state = place(state, tables[0], into_plus_x)
    state = place(state, tables[3], into_minus_y)
    state = place(state, tables[2], into_plus_y)
    return state


def on_device(position, velocity, history, radius, fluid, tile_list, tile_mask, move_slot):
    for step_no in range(move_slot.shape[0]):
        ghost = jnp.concatenate([position, history, radius[None]], axis=0)
        padded = padded_2(ghost, (("gx", 1), ("gy", 2)), 1)
        force = all_forces(padded, tile_list, tile_mask)
        position, velocity, history = advance(position, velocity, history, radius, fluid, force)
        state = jnp.concatenate([position, velocity, history, radius[None]], axis=0)
        state = migrate(state, move_slot[step_no])
        position, velocity, history, radius = (state[0:3], state[3:6], state[6:9], state[9])
    return (position, velocity, history)


def solution(mesh):
    placed = (
        P(None, "gx", "gy", None),
        P(None, "gx", "gy", None),
        P(None, "gx", "gy", None),
        P("gx", "gy", None),
        P(None, "gx", "gy", None),
        P("gx", "gy", None),
        P("gx", "gy", None),
        P(None, "gx", "gy", None),
    )
    return jax.shard_map(
        on_device,
        mesh=mesh,
        in_specs=placed,
        out_specs=(P(None, "gx", "gy", None), P(None, "gx", "gy", None), P(None, "gx", "gy", None)),
        check_vma=False,
    )
```

profile of v0, /device:TPU:1, one launch (start us, length us, event | category | flops | bytes accessed | tf_op | source)
XLA Modules:
  0.0 695.9 jit_solution(4369067634582768668)
XLA Ops:
  1.4 4.0 collective-permute-start
  12.5 4.1 collective-permute-start.2
  18.8 3.1 collective-permute-done.3
  22.1 135.8 %while.44 = (s32[]{:T(128)}, f32[8,3,8,128]{3,2,0,1:T(8,128)S(1)}, s32[8]{0:T(128)S(1)}, f32[7,10,10,128]{3,2,0,1:T(8,128)S(1)}, s32[8,8,4]{1,2,0:T(4,128)S(1)},...) while((s32[]{:T(128)}, f32[8,3,8,128]{3,2,0,1:T(8,128)S(1)}, ...), condition=%wide.region_28.29_spmd.clone, body=%wide.region_0.28_spmd.sunk.clone.sunk | while | flops 41917388 | bytes 20475268 | solution.py:84
  162.9 3.6 collective-permute-start.6
  167.9 5.4 collective-permute-start.4
  176.9 3.4 collective-permute-start.8
  181.6 3.3 collective-permute-done.9
  184.9 4.8 collective-permute-start.10
  191.6 3.3 collective-permute-done.11
  195.1 135.8 %while.45 = (s32[]{:T(128)}, f32[8,3,8,128]{3,2,0,1:T(8,128)S(1)}, s32[8]{0:T(128)S(1)}, f32[7,10,10,128]{3,2,1,0:T(8,128)S(1)}, s32[8,8,4]{1,2,0:T(4,128)S(1)},...) while((s32[]{:T(128)}, f32[8,3,8,128]{3,2,0,1:T(8,128)S(1)}, ...), condition=%wide.region_61.62_spmd.clone, body=%wide.region_33.61_spmd.sunk.clone.sunk | while | flops 41917388 | bytes 20475268 | solution.py:84
  339.7 4.5 collective-permute-start.12
  347.8 3.9 collective-permute-start.16
  353.2 3.4 collective-permute-done.17
  356.7 6.7 collective-permute-start.18
  365.4 3.3 collective-permute-done.19
  368.8 135.8 %while.46 = (s32[]{:T(128)}, f32[8,3,8,128]{3,2,0,1:T(8,128)S(1)}, s32[8]{0:T(128)S(1)}, f32[7,10,10,128]{3,2,1,0:T(8,128)S(1)}, s32[8,8,4]{1,2,0:T(4,128)S(1)},...) while((s32[]{:T(128)}, f32[8,3,8,128]{3,2,0,1:T(8,128)S(1)}, ...), condition=%wide.region_94.95_spmd.clone, body=%wide.region_66.94_spmd.sunk.clone.sunk | while | flops 41917388 | bytes 20475268 | solution.py:84
  513.4 4.3 collective-permute-start.20
  521.3 4.1 collective-permute-start.24
  526.7 3.3 collective-permute-done.25
  530.0 6.8 collective-permute-start.26
  538.9 3.3 collective-permute-done.27
  542.3 135.8 %while.47 = (s32[]{:T(128)}, f32[8,3,8,128]{3,2,0,1:T(8,128)S(1)}, s32[8]{0:T(128)S(1)}, f32[7,10,10,128]{3,2,1,0:T(8,128)S(1)}, s32[8,8,4]{1,2,0:T(4,128)S(1)},...) while((s32[]{:T(128)}, f32[8,3,8,128]{3,2,0,1:T(8,128)S(1)}, ...), condition=%wide.region_127.128_spmd.clone, body=%wide.region_99.127_spmd.sunk.clone.sunk | while | flops 41917388 | bytes 20475268 | solution.py:84
  686.9 4.3 collective-permute-start.28
  (1975 shorter events, 499.9 us)
Async XLA Ops:
  1.4 10.9 %collective-permute-start = (f32[7,1,8,128]{3,2,0,1:T(8,128)S(1)}, f32[7,1,8,128]{3,2,0,1:T(8,128)S(1)}, u32[]{:S(2)}, u32[]{:S(2)}) collective-permute-start(f32[7,1,8,128]{3,2,0,1:T(8,128)S(1)} %get-tuple-element.720), channel_id=1, source_target_pairs={{0,8},{8,16},{16,24},{1,9},{9,17},{17,25},{2,10},{10,18},{18,26},{... | collective-permute-start | bytes 86024 | tf_op jit(solution)/shard_map/ppermute | solution.py:31
  5.5 6.9 collective-permute-start.1
  12.5 6.3 collective-permute-start.2
  160.9 12.5 %collective-permute-start.7 = (f32[10,8,16]{0,2,1:T(8,128)S(1)}, f32[10,8,16]{0,2,1:T(8,128)S(1)}, u32[]{:S(2)}, u32[]{:S(2)}) collective-permute-start(f32[10,8,16]{0,2,1:T(8,128)S(1)} %slice_bitcast_fusion.61), channel_id=1, source_target_pairs={{1,0},{2,1},{3,2},{4,3},{5,4},{6,5},{7,6},{9,8},{10,9},{11,10},{12... | collective-permute-start | bytes 15368 | tf_op jit(solution)/shard_map/ppermute | solution.py:21
  162.9 10.5 %collective-permute-start.6 = (f32[10,8,16]{0,2,1:T(8,128)S(1)}, f32[10,8,16]{0,2,1:T(8,128)S(1)}, u32[]{:S(2)}, u32[]{:S(2)}) collective-permute-start(f32[10,8,16]{0,2,1:T(8,128)S(1)} %slice_bitcast_fusion.60), channel_id=1, source_target_pairs={{0,1},{1,2},{2,3},{3,4},{4,5},{5,6},{6,7},{8,9},{9,10},{10,11},{11... | collective-permute-start | bytes 15368 | tf_op jit(solution)/shard_map/ppermute | solution.py:21
  166.6 8.3 %collective-permute-start.5 = (f32[10,8,16]{0,2,1:T(8,128)S(1)}, f32[10,8,16]{0,2,1:T(8,128)S(1)}, u32[]{:S(2)}, u32[]{:S(2)}) collective-permute-start(f32[10,8,16]{0,2,1:T(8,128)S(1)} %slice_bitcast_fusion.63), channel_id=1, source_target_pairs={{8,0},{16,8},{24,16},{9,1},{17,9},{25,17},{10,2},{18,10},{26,18},{... | collective-permute-start | bytes 15368 | tf_op jit(solution)/shard_map/ppermute | solution.py:21
  167.9 7.0 %collective-permute-start.4 = (f32[10,8,16]{0,2,1:T(8,128)S(1)}, f32[10,8,16]{0,2,1:T(8,128)S(1)}, u32[]{:S(2)}, u32[]{:S(2)}) collective-permute-start(f32[10,8,16]{0,2,1:T(8,128)S(1)} %slice_bitcast_fusion.62), channel_id=1, source_target_pairs={{0,8},{8,16},{16,24},{1,9},{9,17},{17,25},{2,10},{10,18},{18,26},{... | collective-permute-start | bytes 15368 | tf_op jit(solution)/shard_map/ppermute | solution.py:21
  184.9 6.7 collective-permute-start.10
  334.0 10.2 %collective-permute-start.14 = (f32[10,8,16]{0,2,1:T(8,128)S(1)}, f32[10,8,16]{0,2,1:T(8,128)S(1)}, u32[]{:S(2)}, u32[]{:S(2)}) collective-permute-start(f32[10,8,16]{0,2,1:T(8,128)S(1)} %slice_bitcast_fusion.56), channel_id=1, source_target_pairs={{0,1},{1,2},{2,3},{3,4},{4,5},{5,6},{6,7},{8,9},{9,10},{10,11},{11... | collective-permute-start | bytes 15368 | tf_op jit(solution)/shard_map/ppermute | solution.py:21
  335.9 8.3 %collective-permute-start.15 = (f32[10,8,16]{0,2,1:T(8,128)S(1)}, f32[10,8,16]{0,2,1:T(8,128)S(1)}, u32[]{:S(2)}, u32[]{:S(2)}) collective-permute-start(f32[10,8,16]{0,2,1:T(8,128)S(1)} %slice_bitcast_fusion.57), channel_id=1, source_target_pairs={{1,0},{2,1},{3,2},{4,3},{5,4},{6,5},{7,6},{9,8},{10,9},{11,10},{12... | collective-permute-start | bytes 15368 | tf_op jit(solution)/shard_map/ppermute | solution.py:21
  338.4 7.3 %collective-permute-start.13 = (f32[10,8,16]{0,2,1:T(8,128)S(1)}, f32[10,8,16]{0,2,1:T(8,128)S(1)}, u32[]{:S(2)}, u32[]{:S(2)}) collective-permute-start(f32[10,8,16]{0,2,1:T(8,128)S(1)} %slice_bitcast_fusion.59), channel_id=1, source_target_pairs={{8,0},{16,8},{24,16},{9,1},{17,9},{25,17},{10,2},{18,10},{26,18},{... | collective-permute-start | bytes 15368 | tf_op jit(solution)/shard_map/ppermute | solution.py:21
  339.7 6.1 collective-permute-start.12
  347.8 5.4 collective-permute-start.16
  356.7 8.7 %collective-permute-start.18 = (f32[7,10,1,128]{3,2,1,0:T(1,128)S(1)}, f32[7,10,1,128]{3,2,1,0:T(1,128)S(1)}, u32[]{:S(2)}, u32[]{:S(2)}) collective-permute-start(f32[7,10,1,128]{3,2,1,0:T(1,128)S(1)} %get-tuple-element.708), channel_id=1, source_target_pairs={{0,1},{1,2},{2,3},{3,4},{4,5},{5,6},{6,7},{8,9},{9,10},{10,11},{11... | collective-permute-start | bytes 107528 | tf_op jit(solution)/shard_map/ppermute | solution.py:31
  507.7 10.0 %collective-permute-start.22 = (f32[10,8,16]{0,2,1:T(8,128)S(1)}, f32[10,8,16]{0,2,1:T(8,128)S(1)}, u32[]{:S(2)}, u32[]{:S(2)}) collective-permute-start(f32[10,8,16]{0,2,1:T(8,128)S(1)} %slice_bitcast_fusion.52), channel_id=1, source_target_pairs={{0,1},{1,2},{2,3},{3,4},{4,5},{5,6},{6,7},{8,9},{9,10},{10,11},{11... | collective-permute-start | bytes 15368 | tf_op jit(solution)/shard_map/ppermute | solution.py:21
  509.6 8.1 %collective-permute-start.23 = (f32[10,8,16]{0,2,1:T(8,128)S(1)}, f32[10,8,16]{0,2,1:T(8,128)S(1)}, u32[]{:S(2)}, u32[]{:S(2)}) collective-permute-start(f32[10,8,16]{0,2,1:T(8,128)S(1)} %slice_bitcast_fusion.53), channel_id=1, source_target_pairs={{1,0},{2,1},{3,2},{4,3},{5,4},{6,5},{7,6},{9,8},{10,9},{11,10},{12... | collective-permute-start | bytes 15368 | tf_op jit(solution)/shard_map/ppermute | solution.py:21
  512.1 7.1 %collective-permute-start.21 = (f32[10,8,16]{0,2,1:T(8,128)S(1)}, f32[10,8,16]{0,2,1:T(8,128)S(1)}, u32[]{:S(2)}, u32[]{:S(2)}) collective-permute-start(f32[10,8,16]{0,2,1:T(8,128)S(1)} %slice_bitcast_fusion.55), channel_id=1, source_target_pairs={{8,0},{16,8},{24,16},{9,1},{17,9},{25,17},{10,2},{18,10},{26,18},{... | collective-permute-start | bytes 15368 | tf_op jit(solution)/shard_map/ppermute | solution.py:21
  513.4 5.9 collective-permute-start.20
  521.3 5.4 collective-permute-start.24
  530.0 8.8 %collective-permute-start.26 = (f32[7,10,1,128]{3,2,1,0:T(1,128)S(1)}, f32[7,10,1,128]{3,2,1,0:T(1,128)S(1)}, u32[]{:S(2)}, u32[]{:S(2)}) collective-permute-start(f32[7,10,1,128]{3,2,1,0:T(1,128)S(1)} %get-tuple-element.706), channel_id=1, source_target_pairs={{0,1},{1,2},{2,3},{3,4},{4,5},{5,6},{6,7},{8,9},{9,10},{10,11},{11... | collective-permute-start | bytes 107528 | tf_op jit(solution)/shard_map/ppermute | solution.py:31
  681.2 10.0 %collective-permute-start.30 = (f32[10,8,16]{0,2,1:T(8,128)S(1)}, f32[10,8,16]{0,2,1:T(8,128)S(1)}, u32[]{:S(2)}, u32[]{:S(2)}) collective-permute-start(f32[10,8,16]{0,2,1:T(8,128)S(1)} %slice_bitcast_fusion.48), channel_id=1, source_target_pairs={{0,1},{1,2},{2,3},{3,4},{4,5},{5,6},{6,7},{8,9},{9,10},{10,11},{11... | collective-permute-start | bytes 15368 | tf_op jit(solution)/shard_map/ppermute | solution.py:21
  683.1 8.1 %collective-permute-start.31 = (f32[10,8,16]{0,2,1:T(8,128)S(1)}, f32[10,8,16]{0,2,1:T(8,128)S(1)}, u32[]{:S(2)}, u32[]{:S(2)}) collective-permute-start(f32[10,8,16]{0,2,1:T(8,128)S(1)} %slice_bitcast_fusion.49), channel_id=1, source_target_pairs={{1,0},{2,1},{3,2},{4,3},{5,4},{6,5},{7,6},{9,8},{10,9},{11,10},{12... | collective-permute-start | bytes 15368 | tf_op jit(solution)/shard_map/ppermute | solution.py:21
  685.6 7.1 %collective-permute-start.29 = (f32[10,8,16]{0,2,1:T(8,128)S(1)}, f32[10,8,16]{0,2,1:T(8,128)S(1)}, u32[]{:S(2)}, u32[]{:S(2)}) collective-permute-start(f32[10,8,16]{0,2,1:T(8,128)S(1)} %slice_bitcast_fusion.51), channel_id=1, source_target_pairs={{8,0},{16,8},{24,16},{9,1},{17,9},{25,17},{10,2},{18,10},{26,18},{... | collective-permute-start | bytes 15368 | tf_op jit(solution)/shard_map/ppermute | solution.py:21
  686.9 5.9 collective-permute-start.28
  (19 other events, 627.5 us)
where the time goes:
time: 705 us; the launch traced here: 696 us
  other arithmetic  244 us (35%)
  matrix products  171 us (24%)
  loops' own time  110 us (16%)
  starting transfers between devices  92.9 us (13%)
  local copies, waits for them, and re-layouts  50.8 us (7%)
  waiting for transfers between devices  23.3 us (3%)
    dot_general x160, matrix products, pair_forces(): jnp.einsum('bij,cbj->cbi', intersection, far_his, precision=lax.Precision...  148 us
    reduce_sum x64, other arithmetic, pair_forces(): pushing = jnp.sum(intersection[None] * delta / distance[None], axis=3)  130 us
    another operation x4, loops' own time, all_forces(): result = lax.map(one_row, jnp.arange(rows, dtype=jnp.int32))  110 us
    reduce_sum x64, other arithmetic, pair_forces(): loading = jnp.sum(intersection, axis=2)  61.9 us
    ppermute x16, starting transfers between devices, from_behind(): lax.ppermute(value, axis, [(source, source + steps) for source in range(f...  42.1 us
    ppermute x8, starting transfers between devices, padded_2(): before = lax.ppermute(last, axis, up)  37.8 us
    ppermute x8, waiting for transfers between devices, padded_2(): after = lax.ppermute(first, axis, down)  23 us
    dynamic_slice x32, local copies, waits for them, and re-layouts, all_forces(): result = lax.map(one_row, jnp.arange(rows, dtype=jnp.int32))  18.8 us
  transfers between devices with their start and end apart: 32, of which 9 were waited for; matrix products, arithmetic and copies ran while one was open for 2% of the time, Pallas kernels for 0%

commit v1 on v0

v1 whole, which is shorter than its diff:
```python
import functools

import jax
import jax.numpy as jnp
from jax import lax
from jax.experimental import pallas as pl
from jax.experimental.pallas import tpu as pltpu
from jax.sharding import PartitionSpec as P

time_step = 0.05
normal_stiff = 50.0
shear_stiff = 40.0
drag_rate = 2.0
gravity = 1.0
floor_square = 0.0025
base_radius = 0.075
centre = 0.5
absent = -1.0e9
TILE = 16
MESH = pl.DeviceIdType.MESH
f32 = jnp.float32
bf16 = jnp.bfloat16


def pieces(x):
    high = x.astype(bf16).astype(f32)
    rest = x - high
    mid = rest.astype(bf16).astype(f32)
    low = (rest - mid).astype(bf16).astype(f32)
    return high, mid, low


def kernel(
    sizes, pos, vel, his, rad, fluid, slot, inv, listed, masked, pos_out, vel_out, his_out,
    state, packet, left, value, radb, drag, send_edge, land_edge, send_corner, land_corner,
    send_sem, recv_sem,
):
    size_x, size_y, rows, cols, steps, near = sizes
    wide = cols + 2
    high = rows + 2
    me_x = lax.axis_index("gx")
    me_y = lax.axis_index("gy")
    ahead_x, behind_x = lax.rem(me_x + 1, size_x), lax.rem(me_x + size_x - 1, size_x)
    ahead_y, behind_y = lax.rem(me_y + 1, size_y), lax.rem(me_y + size_y - 1, size_y)
    targets = [
        (ahead_x, me_y), (behind_x, me_y), (me_x, ahead_y), (me_x, behind_y),
        (ahead_x, ahead_y), (ahead_x, behind_y), (behind_x, ahead_y), (behind_x, behind_y),
    ]
    has_ahead_x, has_behind_x = me_x < size_x - 1, me_x > 0
    has_ahead_y, has_behind_y = me_y < size_y - 1, me_y > 0

    barrier = pltpu.get_barrier_semaphore()
    for target in targets:
        pl.semaphore_signal(barrier, inc=1, device_id=target, device_id_type=MESH)

    row8 = lax.broadcasted_iota(jnp.int32, (8, 128), 0)

    def load_row(a, _):
        first = ((a + 1) * wide + 1) * TILE
        for c in range(3):
            state[pl.ds(first + c, cols, stride=TILE), :] = pos[c, a]
            state[pl.ds(first + 5 + c, cols, stride=TILE), :] = his[c, a]
            state[pl.ds(first + 8 + c, cols, stride=TILE), :] = vel[c, a]
            drag[pl.ds(a * cols * 8 + c, cols, stride=8), :] = fluid[c, a]
        state[pl.ds(first + 3, cols, stride=TILE), :] = rad[a]
        zero = jnp.zeros((cols, 128), f32)
        for c in (4, 11, 12, 13, 14, 15):
            state[pl.ds(first + c, cols, stride=TILE), :] = zero
        return 0

    lax.fori_loop(0, rows, load_row, 0)

    def copies(x):
        out = []
        for d in range(8):
            source, landing, k = (
                (send_edge, land_edge, d) if d < 4 else (send_corner, land_corner, d - 4)
            )
            out.append(
                pltpu.make_async_remote_copy(
                    src_ref=source.at[x, k],
                    dst_ref=landing.at[x, k],
                    send_sem=send_sem.at[x, d],
                    recv_sem=recv_sem.at[x, d],
                    device_id=targets[d],
                    device_id_type=MESH,
                )
            )
        return out

    def block(r, c):
        return pl.ds(pl.multiple_of((r * wide + c) * TILE, TILE), TILE)

    def run(r, c, count):
        return pl.ds(pl.multiple_of((r * wide + c) * TILE, TILE), count * TILE)

    def send(x):
        send_edge[x, 0] = state[run(rows, 1, cols), :]
        send_edge[x, 1] = state[run(1, 1, cols), :]
        for r in range(rows):
            send_edge[x, 2, r * TILE : (r + 1) * TILE] = state[block(r + 1, cols), :]
            send_edge[x, 3, r * TILE : (r + 1) * TILE] = state[block(r + 1, 1), :]
        send_corner[x, 0] = state[block(rows, cols), :]
        send_corner[x, 1] = state[block(rows, 1), :]
        send_corner[x, 2] = state[block(1, cols), :]
        send_corner[x, 3] = state[block(1, 1), :]
        for copy in copies(x):
            copy.start()

    def receive(x):
        for copy in copies(x):
            copy.wait_recv()
        ax, bx = has_ahead_x.astype(f32), has_behind_x.astype(f32)
        ay, by = has_ahead_y.astype(f32), has_behind_y.astype(f32)
        state[run(0, 1, cols), :] = land_edge[x, 0] * bx
        state[run(rows + 1, 1, cols), :] = land_edge[x, 1] * ax
        for r in range(rows):
            state[block(r + 1, 0), :] = land_edge[x, 2, r * TILE : (r + 1) * TILE] * by
            state[block(r + 1, cols + 1), :] = land_edge[x, 3, r * TILE : (r + 1) * TILE] * ay
        state[block(0, 0), :] = land_corner[x, 0] * (bx * by)
        state[block(0, cols + 1), :] = land_corner[x, 1] * (bx * ay)
        state[block(rows + 1, 0), :] = land_corner[x, 2] * (ax * by)
        state[block(rows + 1, cols + 1), :] = land_corner[x, 3] * (ax * ay)

    pl.semaphore_wait(barrier, 8)
    send(0)
    receive(0)

    def features(n):
        tile = state[pl.ds(pl.multiple_of(n * TILE, TILE), 8), :]
        x = jnp.where(row8 < 3, tile - centre, tile)
        norm = jnp.sum(jnp.where(row8 < 3, x * x, 0.0), axis=0, keepdims=True)
        radius = tile[3:4]
        x = jnp.where(row8 == 3, norm, jnp.where(row8 == 4, 1.0, x))
        h, m, l = pieces(x)
        zero = jnp.zeros_like(h)
        seen = jnp.where(row8 == 0, jnp.where(radius > 0.0, radius, absent), 0.0)
        turned = jnp.transpose(
            jnp.concatenate([h, h, m, h, l, m, zero, zero, seen] + [zero] * 7, axis=0)
        )
        left[n] = turned.astype(bf16)
        radb[n] = jnp.broadcast_to(turned[:, 64:65], (128, 128))
        v = jnp.concatenate([h, m, l, zero], axis=0).astype(bf16)
        value[n] = jnp.concatenate([v, v], axis=1)

    def pair_sums(m, home, u, v, row_radius):
        x = home - jnp.where(row8 == 0, u, jnp.where(row8 == 1, v, 0.0))
        norm = jnp.sum(jnp.where(row8 < 3, x * x, 0.0), axis=0, keepdims=True)
        y = jnp.where(
            row8 < 3, -2.0 * x, jnp.where(row8 == 3, 1.0, jnp.where(row8 == 4, norm, 0.0))
        )
        h, mid, l = pieces(y)
        zero = jnp.zeros_like(h)
        right = jnp.concatenate([h, mid, h, l, h, mid, zero, zero], axis=0).astype(bf16)
        square = jnp.dot(left[m][:, 0:64], right, preferred_element_type=f32)
        square = jnp.maximum(square, floor_square)
        over = lax.rsqrt(square)
        s = jnp.maximum((radb[m] + row_radius) - square * over, 0.0)
        q = s * over
        s_high, q_high = s.astype(bf16), q.astype(bf16)
        s_low = (s - s_high.astype(f32)).astype(bf16)
        q_low = (q - q_high.astype(f32)).astype(bf16)
        weights = jnp.concatenate(
            [
                jnp.concatenate([s_high, q_high], axis=1),
                jnp.concatenate([s_low, q_low], axis=1),
            ],
            axis=0,
        )
        sums = jnp.dot(
            value[m], weights, preferred_element_type=f32
        )
        sums = sums[0:8] + sums[8:16] + sums[16:24]
        picked = jnp.where(row8 < 4, sums[:, 128:], sums[:, :128])
        total = jnp.where(row8 < 4, sums[4:5, 128:], sums[4:5, :128])
        return picked - x * total

    def advance(step, a, b):
        n = (a + 1) * wide + b + 1
        here = pl.ds(pl.multiple_of(n * TILE, TILE), TILE)
        tile = state[here, :]
        home = jnp.where(row8 < 3, tile[0:8] - centre, tile[0:8])
        radius = tile[3:4]
        acc = pair_sums(n, home, 0.0, 0.0, radius)
        for e in range(near):
            at = (a * cols + b) * near + e
            picked = listed[at]
            offset = jnp.where(picked >= 4, picked + 1, picked)
            u = jnp.where(offset >= 6, 1, jnp.where(offset >= 3, 0, -1))
            v = offset - 3 * (u + 1) - 1
            row_radius = radius + jnp.where(masked[at] > 0, 0.0, absent)
            acc = acc + pair_sums(
                n + u * wide + v, home, u.astype(f32), v.astype(f32), row_radius
            )
        force = -normal_stiff * acc[0:3] + shear_stiff * acc[5:8]
        lift = normal_stiff * jnp.maximum(radius - tile[2:3], 0.0)
        row3 = lax.broadcasted_iota(jnp.int32, (3, 128), 0)
        force = force + jnp.where(row3 == 2, lift, 0.0)
        ratio = radius / base_radius
        speed = tile[8:11]
        wind = drag[pl.ds(pl.multiple_of((a * cols + b) * 8, 8), 8), :][0:3]
        accel = (
            force / (ratio * ratio * ratio)
            + drag_rate * (wind - speed)
            - jnp.where(row3 == 2, gravity, 0.0)
        )
        speed = speed + time_step * accel
        moved = tile[0:3] + time_step * speed
        spring = tile[5:8] + time_step * speed
        back = inv[step, a, pl.ds(b, 1), :].astype(f32)
        slots = slot[step, a, pl.ds(b, 1), :].astype(f32)
        state[here, :] = jnp.concatenate(
            [moved, radius, back, spring, speed, slots, tile[12:16]], axis=0
        )

    def spread(rows_of, count):
        one = rows_of.reshape(count, 1, 128)
        return jnp.broadcast_to(one, (count, TILE, 128))

    def make_packets(r, c, count):
        tiles = state[run(r, c, count), :].reshape(count, TILE, 128)
        index = spread(tiles[:, 11:12, :], count).astype(jnp.int32).reshape(count * TILE, 128)
        packet[run(r, c, count), :] = jnp.take_along_axis(
            tiles.reshape(count * TILE, 128), index, axis=1, mode="promise_in_bounds"
        )

    def trade(r, c, count, open_x, open_y):
        shape = (count, TILE, 128)
        up = packet[run(jnp.minimum(r + 1, high - 1), c, count), :].reshape(shape)
        down = packet[run(jnp.maximum(r - 1, 0), c, count), :].reshape(shape)
        if c == 0:
            line = packet[run(r, 0, count), :].reshape(shape)
            ahead = jnp.concatenate([line[1:], line[:1]], axis=0)
            behind = jnp.concatenate([line[-1:], line[:-1]], axis=0)
        else:
            ahead = packet[run(r, c + 1, count), :].reshape(shape)
            behind = packet[run(r, c - 1, count), :].reshape(shape)
        lane = lax.broadcasted_iota(jnp.int32, shape, 2)
        line_no = lax.broadcasted_iota(jnp.int32, shape, 1)
        column = lax.broadcasted_iota(jnp.int32, shape, 0) + c
        shift = jnp.where(
            lane < 32,
            jnp.where(line_no == 0, jnp.where(lane < 16, 1.0, -1.0), 0.0),
            jnp.where(line_no == 1, jnp.where(lane < 48, 1.0, -1.0), 0.0),
        )
        arriving = jnp.where(
            lane < 32, jnp.where(lane < 16, up, down), jnp.where(lane < 48, ahead, behind)
        )
        arriving = (arriving + shift).reshape(count * TILE, 128)
        tiles = state[run(r, c, count), :].reshape(shape)
        back = spread(tiles[:, 4:5, :], count).astype(jnp.int32)
        index = jnp.maximum(back, 0).reshape(count * TILE, 128)
        found = jnp.take_along_axis(arriving, index, axis=1, mode="promise_in_bounds")
        flag_y0, flag_y1 = open_y(column)
        allowed = jnp.where(
            back < 32,
            jnp.where(back < 16, open_x[0], open_x[1]),
            jnp.where(back < 48, flag_y0, flag_y1),
        )
        allowed = jnp.where((back >= 0) & (line_no != 4) & (line_no != 11), allowed, 0)
        state[run(r, c, count), :] = jnp.where(
            allowed > 0, found.reshape(shape), tiles
        ).reshape(count * TILE, 128)

    def as_int(flag):
        return jnp.where(flag, 1, 0)

    def substep(step, _):
        def feature_row(r, _):
            for c in range(wide):
                features(r * wide + c)
            return 0

        lax.fori_loop(0, high, feature_row, 0)

        def advance_one(i, _):
            a = i // cols
            advance(step, a, i - a * cols)
            return 0

        lax.fori_loop(0, rows * cols, advance_one, 0)

        def packets_row(r, _):
            make_packets(r, 1, cols)
            return 0

        lax.fori_loop(1, rows + 1, packets_row, 0)

        def inner_row(r, _):
            trade(
                r, 1, cols, (as_int(r < rows), as_int(r > 1)),
                lambda column: (as_int(column < cols), as_int(column > 1)),
            )
            return 0

        lax.fori_loop(1, rows + 1, inner_row, 0)
        send(step + 1)
        receive(step + 1)
        make_packets(0, 0, wide)
        make_packets(rows + 1, 0, wide)

        def side_row(r, _):
            make_packets(r, 0, 1)
            make_packets(r, cols + 1, 1)
            return 0

        lax.fori_loop(1, rows + 1, side_row, 0)
        behind_x_open, ahead_x_open = as_int(has_behind_x), as_int(has_ahead_x)
        behind_y_open, ahead_y_open = as_int(has_behind_y), as_int(has_ahead_y)

        def cross_row(r, _):
            plus = jnp.where(r == 0, behind_x_open, jnp.where(r == rows, ahead_x_open, 0))
            minus = jnp.where(r == 1, behind_x_open, jnp.where(r == rows + 1, ahead_x_open, 0))

            def open_y(column):
                return (
                    jnp.where(
                        column == 0, behind_y_open, jnp.where(column == cols, ahead_y_open, 0)
                    ),
                    jnp.where(
                        column == 1, behind_y_open, jnp.where(column == cols + 1, ahead_y_open, 0)
                    ),
                )

            trade(r, 0, wide, (plus, minus), open_y)
            return 0

        lax.fori_loop(0, high, cross_row, 0)
        return 0

    lax.fori_loop(0, steps, substep, 0)

    def store_row(a, _):
        first = ((a + 1) * wide + 1) * TILE
        for c in range(3):
            pos_out[c, a] = state[pl.ds(first + c, cols, stride=TILE), :]
            his_out[c, a] = state[pl.ds(first + 5 + c, cols, stride=TILE), :]
            vel_out[c, a] = state[pl.ds(first + 8 + c, cols, stride=TILE), :]
        return 0

    lax.fori_loop(0, rows, store_row, 0)

    def drain(x, _):
        for copy in copies(x):
            copy.wait_send()
        return 0

    lax.fori_loop(0, steps + 1, drain, 0)


def on_device(position, velocity, history, radius, fluid, tile_list, tile_mask, move_slot):
    size_x, size_y = lax.axis_size("gx"), lax.axis_size("gy")
    rows, cols, grains = radius.shape
    steps, near = move_slot.shape[0], tile_list.shape[-1]
    count = move_slot.shape[-1] // 4
    order = jnp.arange(4 * count, dtype=jnp.int32)
    hit = move_slot[..., :, None] == jnp.arange(grains, dtype=jnp.int32)
    inverse = jnp.sum(jnp.where(hit, order[:, None] + 1, 0), axis=-2) - 1
    groups = [move_slot[..., k * count : (k + 1) * count] for k in (1, 0, 3, 2)]
    slots = jnp.concatenate(groups + [jnp.zeros_like(move_slot)], axis=-1)
    blocks = (rows + 2) * (cols + 2)
    shape = jax.ShapeDtypeStruct(position.shape, f32)
    vmem = pl.BlockSpec(memory_space=pltpu.VMEM)
    smem = pl.BlockSpec(memory_space=pltpu.SMEM)
    return pl.pallas_call(
        functools.partial(kernel, (size_x, size_y, rows, cols, steps, near)),
        out_shape=(shape, shape, shape),
        in_specs=[vmem] * 7 + [smem] * 2,
        out_specs=(vmem, vmem, vmem),
        scratch_shapes=[
            pltpu.VMEM((blocks * TILE, grains), f32),
            pltpu.VMEM((blocks * TILE, grains), f32),
            pltpu.VMEM((blocks, 128, 128), bf16),
            pltpu.VMEM((blocks, 32, 256), bf16),
            pltpu.VMEM((blocks, 128, 128), f32),
            pltpu.VMEM((rows * cols * 8, grains), f32),
            pltpu.VMEM((steps + 1, 4, max(rows, cols) * TILE, grains), f32),
            pltpu.VMEM((steps + 1, 4, max(rows, cols) * TILE, grains), f32),
            pltpu.VMEM((steps + 1, 4, TILE, grains), f32),
            pltpu.VMEM((steps + 1, 4, TILE, grains), f32),
            pltpu.SemaphoreType.DMA((steps + 1, 8)),
            pltpu.SemaphoreType.DMA((steps + 1, 8)),
        ],
        compiler_params=pltpu.CompilerParams(
            collective_id=0, has_side_effects=True, vmem_limit_bytes=40 * 1024 * 1024
        ),
    )(
        position, velocity, history, radius, fluid, slots, inverse,
        tile_list.reshape(-1), tile_mask.reshape(-1),
    )


def solution(mesh):
    grid = P(None, "gx", "gy", None)
    flat = P("gx", "gy", None)
    return jax.shard_map(
        on_device,
        mesh=mesh,
        in_specs=(grid, grid, grid, flat, grid, flat, flat, grid),
        out_specs=(grid, grid, grid),
        check_vma=False,
    )
```

time: 705 us -> 261 us (0.37); the launches traced: 696 us -> 260 us
  Pallas kernels: 0 us -> 251 us
  other arithmetic: 244 us -> 3.12 us
  matrix products: 171 us -> 0 us
  loops' own time: 110 us -> 0 us
  starting transfers between devices: 92.9 us -> 0 us
  local copies, waits for them, and re-layouts: 50.8 us -> 5.13 us
  waiting for transfers between devices: 23.3 us -> 0 us
    pallas_call x0 -> x1, Pallas kernels: none -> 251 us  [on_device(): pl.pallas_call(functools.partial(kernel, (size_x, size_y, rows, cols, ste...]
    reduce_sum x240 -> x1, other arithmetic: 222 us -> 3.11 us  [on_device(): inverse = jnp.sum(jnp.where(hit, order[:, None] + 1, 0), axis=-2) - 1]
    dot_general x192 -> x0, matrix products: 171 us -> none  [the longest x160 148 us: pair_forces(): jnp.einsum('bij,cbj->cbi', intersection, far_his, precision=lax.Precision...]
    another operation x4 -> x0, loops' own time: 110 us -> none  [all_forces(): result = lax.map(one_row, jnp.arange(rows, dtype=jnp.int32))]
    ppermute x32 -> x0, starting transfers between devices: 92.9 us -> none  [the longest x16 42.1 us: from_behind(): lax.ppermute(value, axis, [(source, source + steps) for source in range(f...]
    ppermute x32 -> x0, waiting for transfers between devices: 23.3 us -> none  [the longest x8 23 us: padded_2(): after = lax.ppermute(first, axis, down)]
    dynamic_slice x32 -> x0, local copies, waits for them, and re-layouts: 18.8 us -> none  [all_forces(): result = lax.map(one_row, jnp.arange(rows, dtype=jnp.int32))]
    another operation x196 -> x0, local copies, waits for them, and re-layouts: 13.4 us -> none  [the longest x160 12.8 us: row_force(): offset_vec = jnp.stack([along_one, along_two, jnp.zeros_like(along_one)])]
  transfers between devices with their start and end apart: 32 -> 0, of which waited for: 9 -> 0; matrix products, arithmetic and copies ran while one was open for 2% -> 0% of each run, Pallas kernels for 0% -> 0%
where the time goes in v1:
time: 261 us; the launch traced here: 260 us
  Pallas kernels  251 us (96%)
  local copies, waits for them, and re-layouts  5.13 us (2%)
  other arithmetic  3.12 us (1%)
    pallas_call x1, Pallas kernels, on_device(): pl.pallas_call(functools.partial(kernel, (size_x, size_y, rows, cols, ste...  251 us

profile of v1, /device:TPU:1, one launch (start us, length us, event | category | flops | bytes accessed | tf_op | source)
XLA Modules:
  0.0 260.2 jit_solution(10839120478573002702)
XLA Ops:
  0.6 1.3 fusion
  2.0 0.0 copy-start.5
  2.0 0.2 concatenate.3.slot
  2.2 0.7 copy-done.5
  2.9 3.1 %select_reduce_fusion = s32[4,8,8,128]{3,2,1,0:T(8,128)S(1)} fusion(s32[64]{0:T(128)S(1)} %iota_add_fusion, s32[4,8,8,64]{3,2,1,0:T(8,128)S(1)} %copy-done.5), kind=kLoop, calls=%fused_computation | loop fusion | flops 6258688 | bytes 196864 | tf_op jit(solution)/shard_map/reduce_sum | solution.py:358
  6.0 0.0 copy-start.1
  6.0 0.0 copy-start.2
  6.0 0.0 copy-start.3
  6.1 0.0 copy-done.6
  6.1 0.0 copy-start
  6.1 0.0 copy-start.4
  6.1 0.1 copy.13
  6.2 0.1 reshape.17.listed
  6.3 0.1 copy.14
  6.5 0.1 reshape.18.masked
  6.6 0.3 copy-done.1
  6.9 0.0 copy-done.2
  7.0 0.0 copy-done.3
  7.0 0.1 copy-done
  7.1 0.0 copy-done.4
  7.1 251.2 %shard_map.103 = (f32[3,8,8,128]{3,2,1,0:T(8,128)S(1)}, f32[3,8,8,128]{3,2,1,0:T(8,128)S(1)}, f32[3,8,8,128]{3,2,1,0:T(8,128)S(1)}) custom-call(f32[3,8,8,128]{3,2,1,0:T(8,128)S(1)} %copy-done, f32[3,8,8,128]{3,2,1,0:T(8,128)S(1)} %copy-done.1, f32[3,8,8,128]{3,2,1,0:T(8,128)S(1)} %copy-done.2, f32[8,8,128]{2,1,0:T(8,128)S(1)} %copy-done.4, ...), custom_call_target="tpu_custom_call" | custom-call | tf_op jit(solution)/shard_map/pallas_call | solution.py:365
  258.2 0.6 copy.18
  258.9 0.6 copy.19
  259.5 0.6 copy.20
  (6 shorter events, 0.0 us)
Async XLA Ops:
  2.0 0.9 copy-start.5
  2.9 3.2 %copy-start.6 = (s32[8,8,4]{1,2,0:T(4,128)S(1)}, s32[8,8,4]{1,2,0:T(4,128)}, u32[]{:S(2)}) copy-start(s32[8,8,4]{1,2,0:T(4,128)} %param.13) | copy-start | bytes 3076
  2.9 3.4 %copy-start.7 = (s32[8,8,4]{1,2,0:T(4,128)S(1)}, s32[8,8,4]{1,2,0:T(4,128)}, u32[]{:S(2)}) copy-start(s32[8,8,4]{1,2,0:T(4,128)} %param.14) | copy-start | bytes 3076
  6.0 0.9 copy-start.1
  6.0 0.9 copy-start.2
  6.0 1.0 copy-start.3
  6.1 1.0 copy-start
  6.1 1.0 copy-start.4

commit v2 on v1

--- a/solution.py
+++ b/solution.py
@@ -50,8 +50,18 @@
     has_ahead_y, has_behind_y = me_y < size_y - 1, me_y > 0
 
     barrier = pltpu.get_barrier_semaphore()
-    for target in targets:
-        pl.semaphore_signal(barrier, inc=1, device_id=target, device_id_type=MESH)
+    present = [
+        has_ahead_x, has_behind_x, has_ahead_y, has_behind_y,
+        has_ahead_x & has_ahead_y, has_ahead_x & has_behind_y,
+        has_behind_x & has_ahead_y, has_behind_x & has_behind_y,
+    ]
+    opposite = [1, 0, 3, 2, 7, 6, 5, 4]
+    for target, there in zip(targets, present):
+
+        @pl.when(there)
+        def _():
+            pl.semaphore_signal(barrier, inc=1, device_id=target, device_id_type=MESH)
+
 
     row8 = lax.broadcasted_iota(jnp.int32, (8, 128), 0)
 
@@ -104,27 +114,36 @@
         send_corner[x, 1] = state[block(rows, 1), :]
         send_corner[x, 2] = state[block(1, cols), :]
         send_corner[x, 3] = state[block(1, 1), :]
-        for copy in copies(x):
-            copy.start()
+        for copy, there in zip(copies(x), present):
+
+            @pl.when(there)
+            def _():
+                copy.start()
+
 
     def receive(x):
-        for copy in copies(x):
-            copy.wait_recv()
-        ax, bx = has_ahead_x.astype(f32), has_behind_x.astype(f32)
-        ay, by = has_ahead_y.astype(f32), has_behind_y.astype(f32)
-        state[run(0, 1, cols), :] = land_edge[x, 0] * bx
-        state[run(rows + 1, 1, cols), :] = land_edge[x, 1] * ax
+        for d, copy in enumerate(copies(x)):
+
+            @pl.when(present[opposite[d]])
+            def _():
+                copy.wait_recv()
+
+        def kept(landed, d):
+            return jnp.where(present[opposite[d]], landed, 0.0)
+
+        state[run(0, 1, cols), :] = kept(land_edge[x, 0], 0)
+        state[run(rows + 1, 1, cols), :] = kept(land_edge[x, 1], 1)
         for r in range(rows):
-            state[block(r + 1, 0), :] = land_edge[x, 2, r * TILE : (r + 1) * TILE] * by
-            state[block(r + 1, cols + 1), :] = land_edge[x, 3, r * TILE : (r + 1) * TILE] * ay
-        state[block(0, 0), :] = land_corner[x, 0] * (bx * by)
-        state[block(0, cols + 1), :] = land_corner[x, 1] * (bx * ay)
-        state[block(rows + 1, 0), :] = land_corner[x, 2] * (ax * by)
-        state[block(rows + 1, cols + 1), :] = land_corner[x, 3] * (ax * ay)
-
-    pl.semaphore_wait(barrier, 8)
+            part = slice(r * TILE, (r + 1) * TILE)
+            state[block(r + 1, 0), :] = kept(land_edge[x, 2, part], 2)
+            state[block(r + 1, cols + 1), :] = kept(land_edge[x, 3, part], 3)
+        state[block(0, 0), :] = kept(land_corner[x, 0], 4)
+        state[block(0, cols + 1), :] = kept(land_corner[x, 1], 5)
+        state[block(rows + 1, 0), :] = kept(land_corner[x, 2], 6)
+        state[block(rows + 1, cols + 1), :] = kept(land_corner[x, 3], 7)
+
+    pl.semaphore_wait(barrier, sum(jnp.where(there, 1, 0) for there in present))
     send(0)
-    receive(0)
 
     def features(n):
         tile = state[pl.ds(pl.multiple_of(n * TILE, TILE), 8), :]
@@ -135,66 +154,97 @@
         h, m, l = pieces(x)
         zero = jnp.zeros_like(h)
         seen = jnp.where(row8 == 0, jnp.where(radius > 0.0, radius, absent), 0.0)
+        moved = flat_rows(h, m, l)
+        moved = jnp.where(row8 == 6, 1.0, moved)
         turned = jnp.transpose(
-            jnp.concatenate([h, h, m, h, l, m, zero, zero, seen] + [zero] * 7, axis=0)
+            jnp.concatenate([h, h, m, h, l, m, moved, zero + 1.0, seen] + [zero] * 7, axis=0)
         )
         left[n] = turned.astype(bf16)
         radb[n] = jnp.broadcast_to(turned[:, 64:65], (128, 128))
         v = jnp.concatenate([h, m, l, zero], axis=0).astype(bf16)
         value[n] = jnp.concatenate([v, v], axis=1)
 
-    def pair_sums(m, home, u, v, row_radius):
-        x = home - jnp.where(row8 == 0, u, jnp.where(row8 == 1, v, 0.0))
-        norm = jnp.sum(jnp.where(row8 < 3, x * x, 0.0), axis=0, keepdims=True)
-        y = jnp.where(
-            row8 < 3, -2.0 * x, jnp.where(row8 == 3, 1.0, jnp.where(row8 == 4, norm, 0.0))
-        )
-        h, mid, l = pieces(y)
-        zero = jnp.zeros_like(h)
-        right = jnp.concatenate([h, mid, h, l, h, mid, zero, zero], axis=0).astype(bf16)
-        square = jnp.dot(left[m][:, 0:64], right, preferred_element_type=f32)
-        square = jnp.maximum(square, floor_square)
-        over = lax.rsqrt(square)
-        s = jnp.maximum((radb[m] + row_radius) - square * over, 0.0)
-        q = s * over
-        s_high, q_high = s.astype(bf16), q.astype(bf16)
-        s_low = (s - s_high.astype(f32)).astype(bf16)
-        q_low = (q - q_high.astype(f32)).astype(bf16)
-        weights = jnp.concatenate(
-            [
-                jnp.concatenate([s_high, q_high], axis=1),
-                jnp.concatenate([s_low, q_low], axis=1),
-            ],
-            axis=0,
-        )
-        sums = jnp.dot(
-            value[m], weights, preferred_element_type=f32
-        )
-        sums = sums[0:8] + sums[8:16] + sums[16:24]
-        picked = jnp.where(row8 < 4, sums[:, 128:], sums[:, :128])
-        total = jnp.where(row8 < 4, sums[4:5, 128:], sums[4:5, :128])
-        return picked - x * total
-
-    def advance(step, a, b):
+    def flat_rows(h, m, l):
+        out = jnp.zeros_like(h)
+        for k, part in enumerate((h, m, l)):
+            out = jnp.where(row8 == k, part[0:1], out)
+            out = jnp.where(row8 == k + 3, part[1:2], out)
+        return out
+
+    lane8 = lax.broadcasted_iota(jnp.int32, (TILE, 128), 1)
+    row32 = lax.broadcasted_iota(jnp.int32, (32, 256), 0)
+
+    def partners(a, b):
         n = (a + 1) * wide + b + 1
-        here = pl.ds(pl.multiple_of(n * TILE, TILE), TILE)
-        tile = state[here, :]
-        home = jnp.where(row8 < 3, tile[0:8] - centre, tile[0:8])
-        radius = tile[3:4]
-        acc = pair_sums(n, home, 0.0, 0.0, radius)
+        out = [(n, None, None, None)]
         for e in range(near):
             at = (a * cols + b) * near + e
             picked = listed[at]
             offset = jnp.where(picked >= 4, picked + 1, picked)
             u = jnp.where(offset >= 6, 1, jnp.where(offset >= 3, 0, -1))
             v = offset - 3 * (u + 1) - 1
-            row_radius = radius + jnp.where(masked[at] > 0, 0.0, absent)
-            acc = acc + pair_sums(
-                n + u * wide + v, home, u.astype(f32), v.astype(f32), row_radius
-            )
-        force = -normal_stiff * acc[0:3] + shear_stiff * acc[5:8]
+            off = jnp.where(masked[at] > 0, 0.0, absent)
+            out.append((n + u * wide + v, u.astype(f32), v.astype(f32), off))
+        return out
+
+    def squares(a, b):
+        n = (a + 1) * wide + b + 1
+        tile = state[pl.ds(pl.multiple_of(n * TILE, TILE), 8), :]
+        x = jnp.where(row8 < 3, tile - centre, 0.0)
+        norm = jnp.sum(x * x, axis=0, keepdims=True)
+        y = jnp.where(row8 < 3, -2.0 * x, jnp.where(row8 == 3, 1.0, 0.0))
+        y = jnp.where(row8 == 4, norm, y)
+        h, m, l = pieces(y)
+        two = jnp.where(row8 < 6, 2.0, jnp.where(row8 == 6, 1.0, 0.0))
+        right = jnp.concatenate([h, m, h, l, h, m, two, flat_rows(h, m, l)], axis=0).astype(bf16)
+        far = []
+        for m, u, v, _ in partners(a, b):
+            if u is None:
+                scale = jnp.where(lane8 < 48, 1.0, 0.0)
+            else:
+                scale = jnp.where(lane8 < 48, 1.0, u)
+                scale = jnp.where((lane8 >= 51) & (lane8 < 54), v, scale)
+                scale = jnp.where(lane8 == 54, u * u + v * v, scale)
+                scale = jnp.where(lane8 >= 59, v, scale)
+            scale = jnp.concatenate([scale.astype(bf16)] * (128 // TILE), axis=0)
+            far.append((left[m] * scale)[:, 0:64])
+        far = jnp.concatenate(far, axis=0)
+        return jnp.dot(far, right, preferred_element_type=f32)
+
+    def overlaps(a, b, square):
+        n = (a + 1) * wide + b + 1
+        radius = state[pl.ds(pl.multiple_of(n * TILE, TILE), 8), :][3:4]
+        weights, values = [], []
+        for e, (m, u, v, off) in enumerate(partners(a, b)):
+            row_radius = radius if off is None else radius + off
+            part = jnp.maximum(square[e * 128 : (e + 1) * 128], floor_square)
+            over = lax.rsqrt(part)
+            s = jnp.maximum((radb[m] + row_radius) - part * over, 0.0)
+            q = s * over
+            s_high, q_high = s.astype(bf16), q.astype(bf16)
+            s_low = (s - s_high.astype(f32)).astype(bf16)
+            q_low = (q - q_high.astype(f32)).astype(bf16)
+            weights.append(jnp.concatenate([s_high, q_high], axis=1))
+            weights.append(jnp.concatenate([s_low, q_low], axis=1))
+            mine = value[m]
+            if u is not None:
+                shift = jnp.where(row32 == 12, u, jnp.where(row32 == 20, v, 0.0))
+                mine = mine + shift.astype(bf16)
+            values.append(mine)
+        return jnp.concatenate(values, axis=1), jnp.concatenate(weights, axis=0)
+
+    def advance(step, a, b, sums):
+        n = (a + 1) * wide + b + 1
+        here = pl.ds(pl.multiple_of(n * TILE, TILE), TILE)
+        tile = state[here, :]
+        radius = tile[3:4]
+        row3 = lax.broadcasted_iota(jnp.int32, (3, 128), 0)
+        joined = sums[0:8] + sums[8:16] + sums[16:24]
+        shift = jnp.where(row3 == 0, sums[12:13, 128:], jnp.where(row3 == 1, sums[20:21, 128:], 0.0))
+        push = joined[0:3, 128:] + shift - (tile[0:3] - centre) * sums[4:5, 128:]
+        load = tile[5:8] * sums[4:5, :128] - joined[5:8, :128]
+        force = -normal_stiff * push - shear_stiff * load
         lift = normal_stiff * jnp.maximum(radius - tile[2:3], 0.0)
-        row3 = lax.broadcasted_iota(jnp.int32, (3, 128), 0)
         force = force + jnp.where(row3 == 2, lift, 0.0)
         ratio = radius / base_radius
         speed = tile[8:11]
@@ -265,37 +315,22 @@
     def as_int(flag):
         return jnp.where(flag, 1, 0)
 
-    def substep(step, _):
+    def features_of(first_row, last_row, columns):
         def feature_row(r, _):
-            for c in range(wide):
+            for c in columns:
                 features(r * wide + c)
             return 0
 
-        lax.fori_loop(0, high, feature_row, 0)
-
-        def advance_one(i, _):
-            a = i // cols
-            advance(step, a, i - a * cols)
-            return 0
-
-        lax.fori_loop(0, rows * cols, advance_one, 0)
-
-        def packets_row(r, _):
-            make_packets(r, 1, cols)
-            return 0
-
-        lax.fori_loop(1, rows + 1, packets_row, 0)
-
-        def inner_row(r, _):
-            trade(
-                r, 1, cols, (as_int(r < rows), as_int(r > 1)),
-                lambda column: (as_int(column < cols), as_int(column > 1)),
-            )
-            return 0
-
-        lax.fori_loop(1, rows + 1, inner_row, 0)
-        send(step + 1)
-        receive(step + 1)
+        lax.fori_loop(first_row, last_row, feature_row, 0)
+
+    def advance_blocks(step, group):
+        apart = [squares(*at) for at in group]
+        pairs = [overlaps(*at, square) for at, square in zip(group, apart)]
+        sums = [jnp.dot(v, w, preferred_element_type=f32) for v, w in pairs]
+        for at, total in zip(group, sums):
+            advance(step, *at, total)
+
+    def cross():
         make_packets(0, 0, wide)
         make_packets(rows + 1, 0, wide)
 
@@ -326,9 +361,60 @@
             return 0
 
         lax.fori_loop(0, high, cross_row, 0)
+
+    def substep(step, _):
+        features_of(2, rows, range(2, cols))
+
+        def advance_inner(i, _):
+            for c in range(2, cols - 2, 4):
+                advance_blocks(step, [(i + 2, c + k) for k in range(4)])
+            return 0
+
+        lax.fori_loop(0, rows - 4, advance_inner, 0)
+        receive(step)
+
+        @pl.when(step > 0)
+        def _():
+            cross()
+
+        features_of(0, 2, range(wide))
+        features_of(rows, rows + 2, range(wide))
+        features_of(2, rows, (0, 1, cols, cols + 1))
+        fours = cols // 4
+
+        def advance_ends(i, _):
+            r = i // fours
+            a = r + (rows - 4) * (r // 2)
+            advance_blocks(step, [(a, (i - r * fours) * 4 + k) for k in range(4)])
+            return 0
+
+        def advance_sides(i, _):
+            advance_blocks(step, [(i + 2, b) for b in (0, 1, cols - 2, cols - 1)])
+            return 0
+
+        lax.fori_loop(0, 4 * fours, advance_ends, 0)
+        lax.fori_loop(0, rows - 4, advance_sides, 0)
+
+        def packets_row(r, _):
+            make_packets(r, 1, cols)
+            return 0
+
+        lax.fori_loop(1, rows + 1, packets_row, 0)
+
+        def inner_row(r, _):
+            trade(
+                r, 1, cols, (as_int(r < rows), as_int(r > 1)),
+                lambda column: (as_int(column < cols), as_int(column > 1)),
+            )
+            return 0
+
+        lax.fori_loop(1, rows + 1, inner_row, 0)
+        send(step + 1)
         return 0
 
     lax.fori_loop(0, steps, substep, 0)
+    receive(steps)
+    cross()
 
     def store_row(a, _):
         first = ((a + 1) * wide + 1) * TILE
@@ -341,8 +427,12 @@
     lax.fori_loop(0, rows, store_row, 0)
 
     def drain(x, _):
-        for copy in copies(x):
-            copy.wait_send()
+        for copy, there in zip(copies(x), present):
+
+            @pl.when(there)
+            def _():
+                copy.wait_send()
+
         return 0
 
     lax.fori_loop(0, steps + 1, drain, 0)

time: 261 us -> 121 us (0.46)
  Pallas kernels: 251 us -> 112 us
    pallas_call x1, Pallas kernels: 251 us -> 112 us  [on_device(): pl.pallas_call(functools.partial(kernel, (size_x, size_y, rows, cols, ste...]
where the time goes in v2:
time: 121 us
  Pallas kernels  112 us (93%)
  local copies, waits for them, and re-layouts  5.13 us (4%)
  other arithmetic  3.12 us (3%)
    pallas_call x1, Pallas kernels, on_device(): pl.pallas_call(functools.partial(kernel, (size_x, size_y, rows, cols, ste...  112 us
    unnamed x21, local copies, waits for them, and re-layouts  3.36 us
    reduce_sum x1, other arithmetic, on_device(): inverse = jnp.sum(jnp.where(hit, order[:, None] + 1, 0), axis=-2) - 1  3.11 us

profile of v2, /device:TPU:1, one launch (start us, length us, event | category | flops | bytes accessed | tf_op | source)
XLA Modules:
  0.0 121.1 jit_solution(288632491772843693)
XLA Ops:
  0.6 1.3 %fusion = (s32[4,8,8,16]{3,2,1,0:T(8,128)S(1)}, s32[4,8,8,16]{3,2,1,0:T(8,128)S(1)}, s32[4,8,8,16]{3,2,1,0:T(8,128)S(1)}, s32[4,8,8,16]{3,2,1,0:T(8,128)S(1)}) fusion(s32[4,8,8,64]{3,2,1,0:T(8,128)} %param.15), kind=kLoop, calls=%fused_computation.4 | loop fusion | bytes 131072 | tf_op jit(solution)/shard_map/slice | solution.py:449
  2.0 0.0 copy-start.5
  2.0 0.2 concatenate.3.slot
  2.2 0.7 copy-done.5
  2.9 3.1 %select_reduce_fusion = s32[4,8,8,128]{3,2,1,0:T(8,128)S(1)} fusion(s32[64]{0:T(128)S(1)} %iota_add_fusion, s32[4,8,8,64]{3,2,1,0:T(8,128)S(1)} %copy-done.5), kind=kLoop, calls=%fused_computation | loop fusion | flops 6258688 | bytes 196864 | tf_op jit(solution)/shard_map/reduce_sum | solution.py:448
  6.0 0.0 copy-start.1
  6.0 0.0 copy-start.2
  6.0 0.0 copy-start.3
  6.1 0.0 copy-done.6
  6.1 0.0 copy-start
  6.1 0.0 copy-start.4
  6.1 0.1 copy.13
  6.2 0.1 reshape.17.listed
  6.3 0.1 copy.14
  6.5 0.1 reshape.18.masked
  6.6 0.3 copy-done.1
  6.9 0.0 copy-done.2
  7.0 0.0 copy-done.3
  7.0 0.1 copy-done
  7.1 0.0 copy-done.4
  7.1 112.1 %shard_map.103 = (f32[3,8,8,128]{3,2,1,0:T(8,128)S(1)}, f32[3,8,8,128]{3,2,1,0:T(8,128)S(1)}, f32[3,8,8,128]{3,2,1,0:T(8,128)S(1)}) custom-call(f32[3,8,8,128]{3,2,1,0:T(8,128)S(1)} %copy-done, f32[3,8,8,128]{3,2,1,0:T(8,128)S(1)} %copy-done.1, f32[3,8,8,128]{3,2,1,0:T(8,128)S(1)} %copy-done.2, f32[8,8,128]{2,1,0:T(8,128)S(1)} %copy-done.4, ...), custom_call_target="tpu_custom_call" | custom-call | tf_op jit(solution)/shard_map/pallas_call | solution.py:455
  119.2 0.6 copy.18
  119.8 0.6 copy.19
  120.5 0.6 copy.20
  (6 shorter events, 0.0 us)
Async XLA Ops:
  2.0 0.9 copy-start.5
  2.9 3.2 %copy-start.6 = (s32[8,8,4]{1,2,0:T(4,128)S(1)}, s32[8,8,4]{1,2,0:T(4,128)}, u32[]{:S(2)}) copy-start(s32[8,8,4]{1,2,0:T(4,128)} %param.13) | copy-start | bytes 3076
  2.9 3.4 %copy-start.7 = (s32[8,8,4]{1,2,0:T(4,128)S(1)}, s32[8,8,4]{1,2,0:T(4,128)}, u32[]{:S(2)}) copy-start(s32[8,8,4]{1,2,0:T(4,128)} %param.14) | copy-start | bytes 3076
  6.0 0.9 copy-start.1
  6.0 0.9 copy-start.2
  6.0 1.0 copy-start.3
  6.1 1.0 copy-start
  6.1 1.0 copy-start.4

commit v3 on v2

--- a/solution.py
+++ b/solution.py
@@ -263,54 +263,65 @@
             [moved, radius, back, spring, speed, slots, tile[12:16]], axis=0
         )
 
-    def spread(rows_of, count):
-        one = rows_of.reshape(count, 1, 128)
-        return jnp.broadcast_to(one, (count, TILE, 128))
-
-    def make_packets(r, c, count):
-        tiles = state[run(r, c, count), :].reshape(count, TILE, 128)
-        index = spread(tiles[:, 11:12, :], count).astype(jnp.int32).reshape(count * TILE, 128)
-        packet[run(r, c, count), :] = jnp.take_along_axis(
-            tiles.reshape(count * TILE, 128), index, axis=1, mode="promise_in_bounds"
-        )
-
-    def trade(r, c, count, open_x, open_y):
-        shape = (count, TILE, 128)
-        up = packet[run(jnp.minimum(r + 1, high - 1), c, count), :].reshape(shape)
-        down = packet[run(jnp.maximum(r - 1, 0), c, count), :].reshape(shape)
-        if c == 0:
-            line = packet[run(r, 0, count), :].reshape(shape)
-            ahead = jnp.concatenate([line[1:], line[:1]], axis=0)
-            behind = jnp.concatenate([line[-1:], line[:-1]], axis=0)
-        else:
-            ahead = packet[run(r, c + 1, count), :].reshape(shape)
-            behind = packet[run(r, c - 1, count), :].reshape(shape)
-        lane = lax.broadcasted_iota(jnp.int32, shape, 2)
-        line_no = lax.broadcasted_iota(jnp.int32, shape, 1)
-        column = lax.broadcasted_iota(jnp.int32, shape, 0) + c
-        shift = jnp.where(
-            lane < 32,
-            jnp.where(line_no == 0, jnp.where(lane < 16, 1.0, -1.0), 0.0),
-            jnp.where(line_no == 1, jnp.where(lane < 48, 1.0, -1.0), 0.0),
-        )
-        arriving = jnp.where(
-            lane < 32, jnp.where(lane < 16, up, down), jnp.where(lane < 48, ahead, behind)
-        )
-        arriving = (arriving + shift).reshape(count * TILE, 128)
-        tiles = state[run(r, c, count), :].reshape(shape)
-        back = spread(tiles[:, 4:5, :], count).astype(jnp.int32)
-        index = jnp.maximum(back, 0).reshape(count * TILE, 128)
-        found = jnp.take_along_axis(arriving, index, axis=1, mode="promise_in_bounds")
-        flag_y0, flag_y1 = open_y(column)
-        allowed = jnp.where(
-            back < 32,
-            jnp.where(back < 16, open_x[0], open_x[1]),
-            jnp.where(back < 48, flag_y0, flag_y1),
-        )
-        allowed = jnp.where((back >= 0) & (line_no != 4) & (line_no != 11), allowed, 0)
-        state[run(r, c, count), :] = jnp.where(
-            allowed > 0, found.reshape(shape), tiles
-        ).reshape(count * TILE, 128)
+    lane = lax.broadcasted_iota(jnp.int32, (8, 128), 1)
+    shift = jnp.where(
+        lane < 32,
+        jnp.where(row8 == 0, jnp.where(lane < 16, 1.0, -1.0), 0.0),
+        jnp.where(row8 == 1, jnp.where(lane < 48, 1.0, -1.0), 0.0),
+    )
+
+    def half(n, k):
+        return pl.ds(pl.multiple_of(n * TILE + 8 * k, 8), 8)
+
+    def gather(x, index):
+        return jnp.take_along_axis(x, index, axis=1, mode="promise_in_bounds")
+
+    def make_packets(r, columns):
+        out = []
+        for c in columns:
+            n = r * wide + c
+            first, second = state[half(n, 0), :], state[half(n, 1), :]
+            index = jnp.broadcast_to(second[3:4], (8, 128)).astype(jnp.int32)
+            out.append((n, gather(first, index), gather(second, index)))
+        for n, first, second in out:
+            packet[half(n, 0), :] = first
+            packet[half(n, 1), :] = second
+
+    def trade(r, columns, flags):
+        out = []
+        for c in columns:
+            n = r * wide + c
+            sides = (
+                jnp.minimum(r + 1, high - 1) * wide + c,
+                jnp.maximum(r - 1, 0) * wide + c,
+                r * wide + min(c + 1, wide - 1),
+                r * wide + max(c - 1, 0),
+            )
+            first, second = state[half(n, 0), :], state[half(n, 1), :]
+            back = jnp.broadcast_to(first[4:5], (8, 128)).astype(jnp.int32)
+            moves = lax.shift_right_logical(
+                jnp.broadcast_to(flags(c), (8, 128)), lax.shift_right_logical(back, 4)
+            )
+            moves = (moves & 1) > 0
+            halves = []
+            for k in range(2):
+                come = [packet[half(side, k), :] for side in sides]
+                come = jnp.where(
+                    lane < 32,
+                    jnp.where(lane < 16, come[0], come[1]),
+                    jnp.where(lane < 48, come[2], come[3]),
+                )
+                halves.append(gather(come + shift if k == 0 else come, back))
+            out.append(
+                (
+                    n,
+                    jnp.where(moves & (row8 != 4), halves[0], first),
+                    jnp.where(moves & (row8 != 3), halves[1], second),
+                )
+            )
+        for n, first, second in out:
+            state[half(n, 0), :] = first
+            state[half(n, 1), :] = second
 
     def as_int(flag):
         return jnp.where(flag, 1, 0)
@@ -324,43 +335,52 @@
         lax.fori_loop(first_row, last_row, feature_row, 0)
 
     def advance_blocks(step, group):
-        apart = [squares(*at) for at in group]
-        pairs = [overlaps(*at, square) for at, square in zip(group, apart)]
-        sums = [jnp.dot(v, w, preferred_element_type=f32) for v, w in pairs]
+        sums = []
+        ahead = squares(*group[0])
+        for k, at in enumerate(group):
+            square = ahead
+            if k + 1 < len(group):
+                ahead = squares(*group[k + 1])
+            mine, weights = overlaps(*at, square)
+            sums.append(jnp.dot(mine, weights, preferred_element_type=f32))
         for at, total in zip(group, sums):
             advance(step, *at, total)
 
     def cross():
-        make_packets(0, 0, wide)
-        make_packets(rows + 1, 0, wide)
+        make_packets(0, range(wide))
+        make_packets(rows + 1, range(wide))
 
         def side_row(r, _):
-            make_packets(r, 0, 1)
-            make_packets(r, cols + 1, 1)
+            make_packets(r, (0, cols + 1))
             return 0
 
         lax.fori_loop(1, rows + 1, side_row, 0)
         behind_x_open, ahead_x_open = as_int(has_behind_x), as_int(has_ahead_x)
         behind_y_open, ahead_y_open = as_int(has_behind_y), as_int(has_ahead_y)
 
-        def cross_row(r, _):
-            plus = jnp.where(r == 0, behind_x_open, jnp.where(r == rows, ahead_x_open, 0))
-            minus = jnp.where(r == 1, behind_x_open, jnp.where(r == rows + 1, ahead_x_open, 0))
-
-            def open_y(column):
-                return (
-                    jnp.where(
-                        column == 0, behind_y_open, jnp.where(column == cols, ahead_y_open, 0)
-                    ),
-                    jnp.where(
-                        column == 1, behind_y_open, jnp.where(column == cols + 1, ahead_y_open, 0)
-                    ),
-                )
-
-            trade(r, 0, wide, (plus, minus), open_y)
-            return 0
-
-        lax.fori_loop(0, high, cross_row, 0)
+        def open_y(c):
+            if c == 0:
+                return 4 * behind_y_open
+            if c == 1:
+                return 8 * behind_y_open
+            if c == cols:
+                return 4 * ahead_y_open
+            return 8 * ahead_y_open if c == cols + 1 else 0
+
+        def end_rows(r, open_x):
+            trade(r, range(wide), lambda c: open_x + open_y(c))
+
+        end_rows(0, behind_x_open)
+        end_rows(1, 2 * behind_x_open)
+        end_rows(rows, ahead_x_open)
+        end_rows(rows + 1, 2 * ahead_x_open)
+
+        def side_rows(i, _):
+            for k in range(2):
+                trade(2 * i + 2 + k, (0, 1, cols, cols + 1), open_y)
+            return 0
+
+        lax.fori_loop(0, (rows - 2) // 2, side_rows, 0)
 
     def substep(step, _):
         features_of(2, rows, range(2, cols))
@@ -382,34 +402,58 @@
         features_of(2, rows, (0, 1, cols, cols + 1))
         fours = cols // 4
 
-        def advance_ends(i, _):
+        def edge_ends(i, _):
             r = i // fours
-            a = r + (rows - 4) * (r // 2)
-            advance_blocks(step, [(a, (i - r * fours) * 4 + k) for k in range(4)])
-            return 0
-
-        def advance_sides(i, _):
-            advance_blocks(step, [(i + 2, b) for b in (0, 1, cols - 2, cols - 1)])
-            return 0
-
-        lax.fori_loop(0, 4 * fours, advance_ends, 0)
-        lax.fori_loop(0, rows - 4, advance_sides, 0)
+            advance_blocks(step, [(r * (rows - 1), (i - r * fours) * 4 + k) for k in range(4)])
+            return 0
+
+        def edge_sides(i, _):
+            advance_blocks(
+                step, [(2 * i + 1 + j, b) for j in range(2) for b in (0, cols - 1)]
+            )
+            return 0
+
+        def next_ends(i, _):
+            advance_blocks(
+                step, [(a, 2 * i + 1 + k) for a in (1, rows - 2) for k in range(2)]
+            )
+            return 0
+
+        def next_sides(i, _):
+            advance_blocks(
+                step, [(2 * i + 2 + j, b) for j in range(2) for b in (1, cols - 2)]
+            )
+            return 0
+
+        lax.fori_loop(0, 2 * fours, edge_ends, 0)
+        lax.fori_loop(0, (rows - 2) // 2, edge_sides, 0)
+
+        @pl.when(step == steps - 1)
+        def _():
+            send(step + 1)
+
+        lax.fori_loop(0, (cols - 2) // 2, next_ends, 0)
+        lax.fori_loop(0, (rows - 4) // 2, next_sides, 0)
 
         def packets_row(r, _):
-            make_packets(r, 1, cols)
+            make_packets(r, range(1, cols + 1))
             return 0
 
         lax.fori_loop(1, rows + 1, packets_row, 0)
 
         def inner_row(r, _):
+            open_x = as_int(r < rows) + 2 * as_int(r > 1)
             trade(
-                r, 1, cols, (as_int(r < rows), as_int(r > 1)),
-                lambda column: (as_int(column < cols), as_int(column > 1)),
+                r, range(1, cols + 1), lambda c: open_x + 4 * int(c < cols) + 8 * int(c > 1)
             )
             return 0
 
         lax.fori_loop(1, rows + 1, inner_row, 0)
-        send(step + 1)
+
+        @pl.when(step < steps - 1)
+        def _():
+            send(step + 1)
+
         return 0
 
     lax.fori_loop(0, steps, substep, 0)
@@ -445,7 +489,7 @@
     count = move_slot.shape[-1] // 4
     order = jnp.arange(4 * count, dtype=jnp.int32)
     hit = move_slot[..., :, None] == jnp.arange(grains, dtype=jnp.int32)
-    inverse = jnp.sum(jnp.where(hit, order[:, None] + 1, 0), axis=-2) - 1
+    inverse = jnp.sum(jnp.where(hit, order[:, None] - 4 * count, 0), axis=-2) + 4 * count
     groups = [move_slot[..., k * count : (k + 1) * count] for k in (1, 0, 3, 2)]
     slots = jnp.concatenate(groups + [jnp.zeros_like(move_slot)], axis=-1)
     blocks = (rows + 2) * (cols + 2)

time: 121 us -> 112 us (0.926)
  Pallas kernels: 112 us -> 103 us
    pallas_call x1, Pallas kernels: 112 us -> 103 us  [on_device(): pl.pallas_call(functools.partial(kernel, (size_x, size_y, rows, cols, ste...]
where the time goes in v3:
time: 112 us
  Pallas kernels  103 us (92%)
  local copies, waits for them, and re-layouts  5.13 us (5%)
  other arithmetic  3.12 us (3%)
    pallas_call x1, Pallas kernels, on_device(): pl.pallas_call(functools.partial(kernel, (size_x, size_y, rows, cols, ste...  103 us
    unnamed x21, local copies, waits for them, and re-layouts  3.36 us
    reduce_sum x1, other arithmetic, on_device(): jnp.sum(jnp.where(hit, order[:, None] - 4 * count, 0), axis=-2) + 4 * count  3.11 us

profile of v3, /device:TPU:1, one launch (start us, length us, event | category | flops | bytes accessed | tf_op | source)
XLA Modules:
  0.0 111.6 jit_solution(3504983247690759885)
XLA Ops:
  0.6 1.3 %fusion = (s32[4,8,8,16]{3,2,1,0:T(8,128)S(1)}, s32[4,8,8,16]{3,2,1,0:T(8,128)S(1)}, s32[4,8,8,16]{3,2,1,0:T(8,128)S(1)}, s32[4,8,8,16]{3,2,1,0:T(8,128)S(1)}) fusion(s32[4,8,8,64]{3,2,1,0:T(8,128)} %param.15), kind=kLoop, calls=%fused_computation.4 | loop fusion | bytes 131072 | tf_op jit(solution)/shard_map/slice | solution.py:493
  2.0 0.0 copy-start.5
  2.0 0.2 concatenate.3.slot
  2.2 0.7 copy-done.5
  2.9 3.1 %select_reduce_fusion = s32[4,8,8,128]{3,2,1,0:T(8,128)S(1)} fusion(s32[64]{0:T(128)S(1)} %iota_add_fusion, s32[4,8,8,64]{3,2,1,0:T(8,128)S(1)} %copy-done.5), kind=kLoop, calls=%fused_computation | loop fusion | flops 6258688 | bytes 196864 | tf_op jit(solution)/shard_map/reduce_sum | solution.py:492
  6.0 0.0 copy-start.1
  6.0 0.0 copy-start.2
  6.0 0.0 copy-start.3
  6.1 0.0 copy-done.6
  6.1 0.0 copy-start
  6.1 0.0 copy-start.4
  6.1 0.1 copy.13
  6.2 0.1 reshape.17.listed
  6.3 0.0 copy-done.7
  6.3 0.1 copy.14
  6.5 0.1 reshape.18.masked
  6.6 0.3 copy-done.1
  6.9 0.0 copy-done.2
  7.0 0.0 copy-done.3
  7.0 0.1 copy-done
  7.1 102.6 %shard_map.103 = (f32[3,8,8,128]{3,2,1,0:T(8,128)S(1)}, f32[3,8,8,128]{3,2,1,0:T(8,128)S(1)}, f32[3,8,8,128]{3,2,1,0:T(8,128)S(1)}) custom-call(f32[3,8,8,128]{3,2,1,0:T(8,128)S(1)} %copy-done, f32[3,8,8,128]{3,2,1,0:T(8,128)S(1)} %copy-done.1, f32[3,8,8,128]{3,2,1,0:T(8,128)S(1)} %copy-done.2, f32[8,8,128]{2,1,0:T(8,128)S(1)} %copy-done.4, ...), custom_call_target="tpu_custom_call" | custom-call | tf_op jit(solution)/shard_map/pallas_call | solution.py:499
  109.7 0.6 copy.18
  110.3 0.6 copy.19
  111.0 0.6 copy.20
  (6 shorter events, 0.0 us)
Async XLA Ops:
  2.0 0.9 copy-start.5
  2.9 3.2 %copy-start.6 = (s32[8,8,4]{1,2,0:T(4,128)S(1)}, s32[8,8,4]{1,2,0:T(4,128)}, u32[]{:S(2)}) copy-start(s32[8,8,4]{1,2,0:T(4,128)} %param.13) | copy-start | bytes 3076
  2.9 3.4 %copy-start.7 = (s32[8,8,4]{1,2,0:T(4,128)S(1)}, s32[8,8,4]{1,2,0:T(4,128)}, u32[]{:S(2)}) copy-start(s32[8,8,4]{1,2,0:T(4,128)} %param.14) | copy-start | bytes 3076
  6.0 0.9 copy-start.1
  6.0 0.9 copy-start.2
  6.0 1.0 copy-start.3
  6.1 1.0 copy-start
  6.1 1.0 copy-start.4
